TPU v7x, 512 devices: a whole 4x4x16 slice. The times are simulated.
512 devices in a mesh: depth: 16 (over x_hi, y, core), tile: 32 (over z, x_lo).
Axes of the slice: x: 4 (x_hi: 2, x_lo: 2; x = x_hi * 2 + x_lo), y: 4, z: 16, core: 2. Of those that a mesh axis runs over, the one named last changes fastest.
Arguments:
- volume: float32 [16, 1024, 1024], P('depth', 'tile'), may hold values from 0.05 to 100
- measured: float32 [1024, 1024], P('tile'), may hold values from 0.15 to 0.6
- point_spread: bfloat16 [16, 13, 13], P('depth'), may hold values from 7.390976e-05 to 0.0007362366
- entry_block: int32 [32, 4096], P('tile', 'depth'), may hold values from 0 to 63
- entry_neuron: int32 [32, 4096], P('tile', 'depth'), may hold values from -1 to 8191, as said below
- footprints: bfloat16 [32, 4096, 4, 128], P('tile', 'depth'), may hold values from 0.049804688 to 1
- seed_plane: int32 [8192], replicated, may hold values from 0 to 15
- seed_row: int32 [8192], replicated, may hold values from 0 to 1023
- seed_col: int32 [8192], replicated, may hold values from 0 to 1023
- owner_slot: int32 [8192], replicated, may hold values from 0 to 8191, each once
Outputs:
- estimate: float32 [16, 1024, 1024], P('depth', 'tile')
- demixed: float32 [8192], P(('depth', 'tile'))
Inputs may be any that keep to these rules, and one draw needn't show every extreme that they name: `entry_neuron`: -1 marks an empty slot; on each device the active slots come first, from 85 to 256 of them, and some device has all 256 slots active; neuron ids may repeat.
All inputs are finite; a program needn't handle non-finite values.
Results may differ from a plain program's by a relative error of at most 0.0025.
Values may be sent and summed in bfloat16 or wider, within the bound.
No kernel may reach another device: no remote copies, remote signals or barrier semaphores. Data moves between devices by JAX's collectives and lax.ppermute only.
A program may use at most 64 MiB of HBM per device.

v0:
```python
import jax
import jax.numpy as jnp
from jax import lax
from jax.sharding import PartitionSpec as P

ITERS = 2
RADIUS = 6
BR = 4
CB = 128


def padded_2(cells, sides, width):
    for axis, dim in sides:
        count = lax.axis_size(axis)
        ends = count - 1
        head = lax.slice_in_dim(cells, 0, width, axis=dim)
        tail = lax.slice_in_dim(cells, cells.shape[dim] - width, cells.shape[dim], axis=dim)
        cells = jnp.concatenate(
            [
                lax.ppermute(tail, axis, [(i, (i + 1) % count) for i in range(ends)]),
                cells,
                lax.ppermute(head, axis, [((i + 1) % count, i) for i in range(ends)]),
            ],
            axis=dim,
        )
    return cells


def band_tables(point_spread):
    kernel_size = point_spread.shape[1]
    radius = kernel_size // 2
    inner = jnp.arange(3 * CB)[:, None, None]
    outer = jnp.arange(CB)[None, :, None]
    tapnum = jnp.arange(kernel_size)[None, None, :]
    ahead_hot = (inner - CB - outer + radius == tapnum).astype(jnp.float32)
    behind_hot = (CB + outer + radius - inner == tapnum).astype(jnp.float32)
    spread_f = point_spread.astype(jnp.float32)
    high = lax.Precision.HIGHEST
    ahead = jnp.einsum("pak,jik->paji", spread_f, ahead_hot, precision=high).astype(jnp.bfloat16)
    behind = jnp.einsum("pak,jik->paji", spread_f, behind_hot, precision=high).astype(jnp.bfloat16)
    return (ahead, behind)


def column_blocks(field):
    shape = field.shape
    blocks = field.reshape(shape[:-1] + (shape[-1] // CB, CB))
    widths = [(0, 0)] * (len(shape) - 1)
    before = jnp.pad(blocks, widths + [(1, 0), (0, 0)])[..., :-1, :]
    after = jnp.pad(blocks, widths + [(0, 1), (0, 0)])[..., 1:, :]
    return jnp.concatenate([before, blocks, after], axis=-1)


def project_ahead(padded, ahead, rows_dev):
    stacked = column_blocks(padded)
    kernel_size = ahead.shape[1]
    summed = None
    for tapnum in range(kernel_size):
        term = jnp.einsum(
            "prnj,pji->rni",
            stacked[:, tapnum : tapnum + rows_dev],
            ahead[:, tapnum],
            preferred_element_type=jnp.float32,
        )
        summed = term if summed is None else summed + term
    return summed.reshape(rows_dev, -1)


def project_behind(padded, behind, rows_dev):
    stacked = column_blocks(padded)
    kernel_size = behind.shape[1]
    last = kernel_size - 1
    summed = None
    for tapnum in range(kernel_size):
        begin = last - tapnum
        term = jnp.einsum(
            "rnj,pji->prni",
            stacked[begin : begin + rows_dev],
            behind[:, tapnum],
            preferred_element_type=jnp.float32,
        )
        summed = term if summed is None else summed + term
    return summed.reshape(behind.shape[0], rows_dev, -1)


def body(
    volume,
    measured,
    point_spread,
    entry_block,
    entry_neuron,
    footprints,
    seed_plane,
    seed_row,
    seed_col,
    owner_slot,
):
    planes_dev, rows_dev, columns = volume.shape
    norm = jnp.sum(point_spread.astype(jnp.float32), axis=(1, 2))
    ahead, behind = band_tables(point_spread)
    estimate = volume
    for sweep in range(ITERS):
        rounded = estimate.astype(jnp.bfloat16)
        padded = padded_2(rounded, (("tile", 1),), RADIUS)
        partial_value = project_ahead(padded, ahead, rows_dev)
        plane_sum = lax.psum(partial_value.astype(jnp.bfloat16), "depth").astype(jnp.float32)
        ratio = (measured / plane_sum).astype(jnp.bfloat16)
        ratio_padded = padded_2(ratio, (("tile", 0),), RADIUS)
        backward = project_behind(ratio_padded, behind, rows_dev)
        estimate = estimate * backward / norm[:, None, None]
    row_groups = rows_dev // BR
    col_groups = columns // CB
    blocked = estimate.reshape(planes_dev, row_groups, BR, col_groups, CB).transpose(0, 1, 3, 2, 4)
    blocked = blocked.reshape(planes_dev * row_groups * col_groups, BR, CB)
    block_ids = entry_block[0]
    neuron = entry_neuron[0]
    weights = footprints[0].astype(jnp.float32)
    active = (neuron >= 0).astype(jnp.float32)
    neurons = seed_plane.shape[0]
    slot_pos = owner_slot[jnp.maximum(neuron, 0)]
    picked = blocked[block_ids]
    slot_proj = jnp.sum(weights * picked, axis=(1, 2)) * active
    proj_dense = jnp.zeros((neurons,), jnp.float32).at[slot_pos].add(slot_proj)
    holder = (seed_plane // planes_dev == lax.axis_index("depth")) & (
        seed_row // rows_dev == lax.axis_index("tile")
    )
    seed_value = estimate[seed_plane % planes_dev, seed_row % rows_dev, seed_col] * holder.astype(
        jnp.float32
    )
    seed_dense = jnp.zeros((neurons,), jnp.float32).at[owner_slot].add(seed_value)
    group = lax.axis_size(("depth", "tile"))
    owned_count = neurons // group
    proj_all, seed_all = lax.psum((proj_dense, seed_dense), ("depth", "tile"))
    offset = lax.axis_index(("depth", "tile")) * owned_count
    proj_own = lax.dynamic_slice_in_dim(proj_all, offset, owned_count, 0)
    seed_own = lax.dynamic_slice_in_dim(seed_all, offset, owned_count, 0)
    scaled = weights * (seed_all[slot_pos] * active)[:, None, None]
    block_count = blocked.shape[0]
    selector = (jnp.arange(block_count)[:, None] == block_ids[None, :]).astype(jnp.float32)
    rebuilt = jnp.dot(
        selector,
        scaled.reshape(scaled.shape[0], BR * CB),
        precision=lax.Precision.HIGHEST,
        preferred_element_type=jnp.float32,
    )
    rebuilt = rebuilt.reshape(block_count, BR, CB)
    slot_over = jnp.sum(weights * rebuilt[block_ids], axis=(1, 2)) * active
    over_dense = jnp.zeros((neurons,), jnp.float32).at[slot_pos].add(slot_over)
    over_own = lax.psum_scatter(over_dense, ("depth", "tile"), scatter_dimension=0, tiled=True)
    demixed = seed_own * proj_own / (over_own + 100.0 * seed_own)
    return (estimate, demixed)


def solution(mesh):
    in_specs = (
        P("depth", "tile", None),
        P("tile", None),
        P("depth", None, None),
        P("tile", "depth"),
        P("tile", "depth"),
        P("tile", "depth", None, None),
        P(),
        P(),
        P(),
        P(),
    )
    out_specs = (P("depth", "tile", None), P(("depth", "tile")))
    return jax.shard_map(body, mesh=mesh, in_specs=in_specs, out_specs=out_specs, check_vma=False)
```

profile of v0, /device:TPU:1, one launch (start us, length us, event | category | flops | bytes accessed | tf_op | source)
XLA Modules:
  0.0 1035.4 jit_solution(12849229935386808176)
XLA Ops:
  7.2 0.9 convert_element_type.84
  8.7 4.5 collective-permute-start
  13.3 1.3 collective-permute-start.1
  14.7 1.6 fusion.7
  16.3 2.7 fusion.173
  19.1 0.9 fusion.6
  20.0 3.2 fusion.172
  23.3 1.7 gather_fusion.1
  29.7 148.9 %all-reduce.14.cloned.1.call-done = bf16[32,1024]{1,0:T(8,128)(2,1)} async-done(((bf16[32,1024]{1,0:T(8,128)(2,1)}), bf16[32,1024]{1,0:T(8,128)(2,1)}) %all-reduce.14.cloned.1.call-update) | async-done | bytes 65552 | tf_op jit(solution)/shard_map/psum | solution.py:105
  179.5 2.3 collective-permute-start.2
  181.9 1.3 collective-permute-start.3
  183.8 3.3 collective-permute-done.3
  187.3 1.2 fusion.41
  188.5 1.2 convolution_add_fusion.35
  193.3 4.4 collective-permute-start.4
  197.7 1.3 collective-permute-start.5
  199.0 3.2 collective-permute-done.5
  206.1 144.1 %all-reduce.16.cloned.1.call-done = bf16[32,1024]{1,0:T(8,128)(2,1)} async-done(((bf16[32,1024]{1,0:T(8,128)(2,1)}), bf16[32,1024]{1,0:T(8,128)(2,1)}) %all-reduce.16.cloned.1.call-update) | async-done | bytes 65552 | tf_op jit(solution)/shard_map/psum | solution.py:105
  351.0 2.2 collective-permute-start.6
  353.2 1.5 collective-permute-start.7
  355.0 3.5 collective-permute-done.7
  362.6 65.0 %gather_fusion = f32[8192]{0:T(1024)S(1)} fusion(f32[1,32,1024]{2,1,0:T(8,128)S(1)} %fusion.44, s32[8192]{0:T(1024)S(1)} %fusion.156), kind=kCustom, calls=%fused_computation | custom fusion | bytes 163840 | tf_op jit(solution)/shard_map/gather | solution.py:126
  427.6 43.2 %scatter_custom_fusion = f32[8192]{0:T(1024)S(1)} fusion(s32[8192]{0:T(1024)S(1)} %compare_select_fusion.2, f32[8192]{0:T(1024)S(1)} %and_select_fusion, f32[]{:T(128)} %constant.76.clone.1), kind=kCustom, calls=%fused_computation.290 | custom fusion | flops 8192 | bytes 32772 | tf_op jit(solution)/shard_map/scatter-add | solution.py:129
  470.9 109.2 %psum.30 = f32[8192]{0:T(1024)S(1)} all-reduce(f32[8192]{0:T(1024)S(1)} %scatter_custom_fusion), channel_id=1, replica_groups=mesh['depth'=16,'tile'=32] {'depth','tile'}, use_global_device_ids=true, to_apply=%region_4.5 | all-reduce | flops 8192 | bytes 65536 | tf_op jit(solution)/shard_map/psum | solution.py:132
  580.1 1.7 gather_fusion.3
  582.6 1.0 gather_fusion.4
  583.6 1.0 gather_fusion.2
  584.6 1.0 fusion.12
  585.6 2.5 scatter_custom_fusion.1
  588.1 2.5 scatter_custom_fusion.2
  590.7 436.9 %all-reduce.18.cloned.1.call-done = (f32[8192]{0:T(1024)}, f32[8192]{0:T(1024)}) async-done(((f32[8192]{0:T(1024)}, f32[8192]{0:T(1024)}), (f32[8192]{0:T(1024)}, f32[8192]{0:T(1024)})) %all-reduce.18.cloned.1.call-update) | async-done | bytes 65552
  1027.6 1.3 fusion.170
  (181 shorter events, 19.8 us)
Async XLA Ops:
  7.2 171.5 %all-reduce.14.cloned.1.call-start = ((), (), s32[]{:S(2)}) async-start(), calls=%async_computation | async-start | bytes 131072 | tf_op jit(solution)/shard_map/psum | solution.py:105
  8.7 16.3 %collective-permute-start = (bf16[1,6,1024]{2,1,0:T(8,128)(2,1)}, bf16[1,6,1024]{2,1,0:T(8,128)(2,1)}, u32[]{:S(2)}, u32[]{:S(2)}) collective-permute-start(bf16[1,6,1024]{2,1,0:T(8,128)(2,1)} %get-tuple-element.46), channel_id=1, source_target_pairs={{0,1},{1,2},{2,3},{3,4},{4,5},{5,6},{6,7},{7,8},{8,9},{9,10},{10,1... | collective-permute-start | bytes 36872 | tf_op jit(solution)/shard_map/ppermute | solution.py:20
  13.3 11.8 %collective-permute-start.1 = (bf16[1,6,1024]{2,1,0:T(8,128)(2,1)}, bf16[1,6,1024]{2,1,0:T(8,128)(2,1)}, u32[]{:S(2)}, u32[]{:S(2)}) collective-permute-start(bf16[1,6,1024]{2,1,0:T(8,128)(2,1)} %get-tuple-element.47), channel_id=1, source_target_pairs={{1,0},{2,1},{3,2},{4,3},{5,4},{6,5},{7,6},{8,7},{9,8},{10,9},{11,1... | collective-permute-start | bytes 36872 | tf_op jit(solution)/shard_map/ppermute | solution.py:22
  16.3 2.7 copy-start.26
  19.0 7.5 copy-start.6
  19.0 7.7 copy-start.4
  20.0 3.3 copy-start.1
  20.0 3.2 copy-start.30
  20.0 5.0 copy-start.25
  20.0 5.0 copy-start.27
  27.8 1.9 copy-start.29
  27.9 150.8 %copy-start.8 = (f32[32,1024]{1,0:T(8,128)S(1)}, f32[32,1024]{1,0:T(8,128)}, u32[]{:S(2)}) copy-start(f32[32,1024]{1,0:T(8,128)} %param.11) | copy-start | bytes 393220
  29.7 320.5 %all-reduce.16.cloned.1.call-start = ((), (), s32[]{:S(2)}) async-start(), calls=%async_computation.1 | async-start | bytes 131072 | tf_op jit(solution)/shard_map/psum | solution.py:105
  179.5 10.2 copy-start.21
  179.5 4.2 collective-permute-start.2
  181.9 5.2 collective-permute-start.3
  187.2 3.1 copy-start.19
  188.5 2.2 copy-start.17
  191.3 1.3 copy-start.2
  192.5 10.3 copy-start.7
  193.3 9.8 copy-start.5
  193.3 5.7 collective-permute-start.4
  197.7 4.5 collective-permute-start.5
  204.2 150.6 %copy-start.3 = (bf16[1,256,4,128]{3,2,1,0:T(4,128)(2,1)S(1)}, bf16[1,256,4,128]{3,2,1,0:T(4,128)(2,1)}, u32[]{:S(2)}) copy-start(bf16[1,256,4,128]{3,2,1,0:T(4,128)(2,1)} %param.15) | copy-start | bytes 786436
  205.3 153.3 %copy-start.24 = (bf16[1,1,384,128]{3,1,2,0:T(2,128)(2,1)S(1)}, bf16[1,1,384,128]{3,1,2,0:T(2,128)(2,1)}, u32[]{:S(2)}) copy-start(bf16[1,1,384,128]{3,1,2,0:T(2,128)(2,1)} %get-tuple-element.18) | copy-start | bytes 294916
  206.0 821.6 %all-reduce.18.cloned.1.call-start = ((), (), s32[]{:S(2)}) async-start(), calls=%async_computation.2 | async-start | bytes 131072
  351.0 3.9 collective-permute-start.6
  353.2 5.2 collective-permute-start.7
  354.8 4.1 copy-start.23
  354.9 4.2 copy-start.22
  362.6 219.9 %copy-start = (f32[1,32,1024]{2,1,0:T(8,128)}, f32[1,32,1024]{2,1,0:T(8,128)S(1)}, u32[]{:S(2)}) copy-start(f32[1,32,1024]{2,1,0:T(8,128)S(1)} %fusion.44) | copy-start | bytes 393220
  362.6 65.0 %copy-start.28 = (s32[8192]{0:T(1024)S(1)}, s32[8192]{0:T(1024)}, u32[]{:S(2)}) copy-start(s32[8192]{0:T(1024)} %param.16) | copy-start | bytes 98308
  (10 other events, 10.5 us)
Sparse Core Ops, SparseCore 0:
  29.8 148.7 all-reduce.13
  206.1 144.0 all-reduce.15
  590.8 436.7 all-reduce.17
where the time goes:
time: 1040 us
  waiting for transfers between devices  740 us (71%)
  blocking collectives  109 us (10%)
  local copies, waits for them, and re-layouts  79.5 us (8%)
  other arithmetic  56.6 us (5%)
  starting transfers between devices  18.9 us (2%)
  matrix products  16.2 us (2%)
  between operations  15.1 us (1%)
    unnamed x4, waiting for transfers between devices  437 us
    psum x2, waiting for transfers between devices, body(): lax.psum(partial_value.astype(jnp.bfloat16), 'depth').astype(jnp.float32)  293 us
    psum x1, blocking collectives, body(): proj_all, seed_all = lax.psum((proj_dense, seed_dense), ('depth', 'tile'))  109 us
    gather x1, local copies, waits for them, and re-layouts, body(): estimate[seed_plane % planes_dev, seed_row % rows_dev, seed_col]  65 us
    scatter-add x1, other arithmetic, body(): jnp.zeros((neurons,), jnp.float32).at[owner_slot].add(seed_value)  43.2 us
  transfers between devices with their start and end apart: 11, of which 6 were waited for; matrix products, arithmetic and copies ran while one was open for 1% of the time, Pallas kernels for 0%

commit v1 on v0

--- a/solution.py
+++ b/solution.py
@@ -102,7 +102,9 @@
         rounded = estimate.astype(jnp.bfloat16)
         padded = padded_2(rounded, (("tile", 1),), RADIUS)
         partial_value = project_ahead(padded, ahead, rows_dev)
-        plane_sum = lax.psum(partial_value.astype(jnp.bfloat16), "depth").astype(jnp.float32)
+        plane_sum = jnp.sum(
+            lax.all_gather(partial_value.astype(jnp.bfloat16), "depth"), axis=0
+        ).astype(jnp.float32)
         ratio = (measured / plane_sum).astype(jnp.bfloat16)
         ratio_padded = padded_2(ratio, (("tile", 0),), RADIUS)
         backward = project_behind(ratio_padded, behind, rows_dev)

time: 1040 us -> 864 us (0.83)
  waiting for transfers between devices: 740 us -> 573 us
    psum x2 -> x0, waiting for transfers between devices: 293 us -> none  [body(): lax.psum(partial_value.astype(jnp.bfloat16), 'depth').astype(jnp.float32)]
    all_gather x0 -> x2, waiting for transfers between devices: none -> 126 us  [body(): lax.all_gather(partial_value.astype(jnp.bfloat16), 'depth')]
where the time goes in v1:
time: 864 us; the launch traced here: 863 us
  waiting for transfers between devices  573 us (66%)
  blocking collectives  107 us (12%)
  local copies, waits for them, and re-layouts  78.7 us (9%)
  other arithmetic  57 us (7%)
  starting transfers between devices  18.3 us (2%)
  between operations  15.2 us (2%)
  matrix products  14.3 us (2%)
    unnamed x4, waiting for transfers between devices  437 us
    all_gather x2, waiting for transfers between devices, body(): lax.all_gather(partial_value.astype(jnp.bfloat16), 'depth')  126 us
    psum x1, blocking collectives, body(): proj_all, seed_all = lax.psum((proj_dense, seed_dense), ('depth', 'tile'))  107 us
    gather x1, local copies, waits for them, and re-layouts, body(): estimate[seed_plane % planes_dev, seed_row % rows_dev, seed_col]  65 us
    scatter-add x1, other arithmetic, body(): jnp.zeros((neurons,), jnp.float32).at[owner_slot].add(seed_value)  43.2 us
  transfers between devices with their start and end apart: 11, of which 6 were waited for; matrix products, arithmetic and copies ran while one was open for 1% of the time, Pallas kernels for 0%

profile of v1, /device:TPU:1, one launch (start us, length us, event | category | flops | bytes accessed | tf_op | source)
XLA Modules:
  0.0 863.3 jit_solution(5181547163482593181)
XLA Ops:
  7.2 0.9 convert_element_type.102
  8.1 3.9 collective-permute-start
  12.1 1.3 collective-permute-start.1
  13.5 1.6 fusion.7
  15.1 2.7 fusion.173
  21.8 0.9 fusion.6
  22.7 3.0 fusion.172
  25.7 64.7 %all-gather.3.cloned.1.call-done = bf16[16,32,1024]{2,1,0:T(8,128)(2,1)} async-done(((bf16[1,32,1024]{2,1,0:T(8,128)(2,1)}), bf16[16,32,1024]{2,1,0:T(8,128)(2,1)}) %all-gather.3.cloned.1.call-update) | async-done | bytes 1048592 | tf_op jit(solution)/shard_map/all_gather | solution.py:106
  90.4 1.4 reduce_sum.51
  92.0 2.3 collective-permute-start.2
  94.3 1.3 collective-permute-start.3
  96.2 3.3 collective-permute-done.3
  103.8 4.3 collective-permute-start.4
  108.0 1.3 collective-permute-start.5
  109.4 3.2 collective-permute-done.5
  116.5 1.7 gather_fusion.1
  118.4 61.2 %all-gather.5.cloned.1.call-done = bf16[16,32,1024]{2,1,0:T(8,128)(2,1)} async-done(((bf16[1,32,1024]{2,1,0:T(8,128)(2,1)}), bf16[16,32,1024]{2,1,0:T(8,128)(2,1)}) %all-gather.5.cloned.1.call-update) | async-done | bytes 1048592 | tf_op jit(solution)/shard_map/all_gather | solution.py:106
  179.6 1.4 reduce_sum.53
  181.1 2.3 collective-permute-start.6
  183.4 1.5 collective-permute-start.7
  185.2 3.5 collective-permute-done.7
  192.8 65.0 %gather_fusion = f32[8192]{0:T(1024)S(1)} fusion(f32[1,32,1024]{2,1,0:T(8,128)S(1)} %fusion.44, s32[8192]{0:T(1024)S(1)} %fusion.156), kind=kCustom, calls=%fused_computation | custom fusion | bytes 163840 | tf_op jit(solution)/shard_map/gather | solution.py:128
  257.8 43.2 %scatter_custom_fusion = f32[8192]{0:T(1024)S(1)} fusion(s32[8192]{0:T(1024)S(1)} %compare_select_fusion.2, f32[8192]{0:T(1024)S(1)} %and_select_fusion, f32[]{:T(128)} %constant.78.clone.1), kind=kCustom, calls=%fused_computation.288 | custom fusion | flops 8192 | bytes 32772 | tf_op jit(solution)/shard_map/scatter-add | solution.py:131
  301.1 106.7 %psum.14 = f32[8192]{0:T(1024)S(1)} all-reduce(f32[8192]{0:T(1024)S(1)} %scatter_custom_fusion), channel_id=1, replica_groups=mesh['depth'=16,'tile'=32] {'depth','tile'}, use_global_device_ids=true, to_apply=%region_4.5 | all-reduce | flops 8192 | bytes 65536 | tf_op jit(solution)/shard_map/psum | solution.py:134
  407.8 1.7 gather_fusion.3
  410.2 1.0 gather_fusion.4
  411.2 1.0 gather_fusion.2
  412.2 1.0 fusion.12
  413.3 2.5 scatter_custom_fusion.1
  415.8 2.5 scatter_custom_fusion.2
  418.4 437.1 %all-reduce.12.cloned.1.call-done = (f32[8192]{0:T(1024)}, f32[8192]{0:T(1024)}) async-done(((f32[8192]{0:T(1024)}, f32[8192]{0:T(1024)}), (f32[8192]{0:T(1024)}, f32[8192]{0:T(1024)})) %all-reduce.12.cloned.1.call-update) | async-done | bytes 65552
  855.5 1.3 fusion.170
  (189 shorter events, 17.2 us)
Async XLA Ops:
  7.2 83.3 %all-gather.3.cloned.1.call-start = ((), (), s32[]{:S(2)}) async-start(), calls=%async_computation | async-start | bytes 1114112 | tf_op jit(solution)/shard_map/all_gather | solution.py:106
  8.1 9.7 %collective-permute-start = (bf16[1,6,1024]{2,1,0:T(8,128)(2,1)S(1)}, bf16[1,6,1024]{2,1,0:T(8,128)(2,1)S(1)}, u32[]{:S(2)}, u32[]{:S(2)}) collective-permute-start(bf16[1,6,1024]{2,1,0:T(8,128)(2,1)S(1)} %get-tuple-element.46), channel_id=1, source_target_pairs={{0,1},{1,2},{2,3},{3,4},{4,5},{5,6},{6,7},{7,8},{8,9},{9,10},{10,1... | collective-permute-start | bytes 36872 | tf_op jit(solution)/shard_map/ppermute | solution.py:20
  12.1 5.8 collective-permute-start.1
  19.9 1.9 copy-start.29
  21.7 157.9 %all-gather.5.cloned.1.call-start = ((), (), s32[]{:S(2)}) async-start(), calls=%async_computation.1 | async-start | bytes 1114112 | tf_op jit(solution)/shard_map/all_gather | solution.py:106
  22.7 69.2 %copy-start.8 = (f32[32,1024]{1,0:T(8,128)S(1)}, f32[32,1024]{1,0:T(8,128)}, u32[]{:S(2)}) copy-start(f32[32,1024]{1,0:T(8,128)} %param.11) | copy-start | bytes 393220
  25.7 75.6 %copy-start.16 = (bf16[1,1,384,128]{3,1,2,0:T(2,128)(2,1)}, bf16[1,1,384,128]{3,1,2,0:T(2,128)(2,1)S(1)}, u32[]{:S(2)}) copy-start(bf16[1,1,384,128]{3,1,2,0:T(2,128)(2,1)S(1)} %get-tuple-element.11) | copy-start | bytes 294916
  91.9 7.8 copy-start.26
  91.9 8.0 copy-start.24
  91.9 8.2 copy-start.22
  92.0 4.2 collective-permute-start.2
  94.3 5.2 collective-permute-start.3
  101.8 1.3 copy-start.2
  102.5 10.2 %copy-start.7 = (bf16[1,1,384,128]{3,1,2,0:T(2,128)(2,1)S(1)}, bf16[1,1,384,128]{3,1,2,0:T(2,128)(2,1)}, u32[]{:S(2)}) copy-start(bf16[1,1,384,128]{3,1,2,0:T(2,128)(2,1)} %copy-done.6) | copy-start | bytes 294916
  102.7 10.2 %copy-start.5 = (bf16[1,1,384,128]{3,1,2,0:T(2,128)(2,1)S(1)}, bf16[1,1,384,128]{3,1,2,0:T(2,128)(2,1)}, u32[]{:S(2)}) copy-start(bf16[1,1,384,128]{3,1,2,0:T(2,128)(2,1)} %copy-done.4) | copy-start | bytes 294916
  103.8 5.6 collective-permute-start.4
  108.0 4.5 collective-permute-start.5
  114.5 2.0 copy-start.33
  114.5 2.0 copy-start.1
  115.0 3.3 copy-start.32
  115.0 3.3 copy-start.28
  115.0 3.3 copy-start.30
  115.5 65.5 %copy-start.9 = (f32[32,1024]{1,0:T(8,128)S(1)}, f32[32,1024]{1,0:T(8,128)}, u32[]{:S(2)}) copy-start(f32[32,1024]{1,0:T(8,128)} %param.11) | copy-start | bytes 393220
  115.7 69.2 %copy-start.3 = (bf16[1,256,4,128]{3,2,1,0:T(4,128)(2,1)S(1)}, bf16[1,256,4,128]{3,2,1,0:T(4,128)(2,1)}, u32[]{:S(2)}) copy-start(bf16[1,256,4,128]{3,2,1,0:T(4,128)(2,1)} %param.15) | copy-start | bytes 786436
  116.4 739.1 %all-reduce.12.cloned.1.call-start = ((), (), s32[]{:S(2)}) async-start(), calls=%async_computation.2 | async-start | bytes 131072
  181.0 7.8 copy-start.27
  181.1 4.0 collective-permute-start.6
  183.4 5.2 collective-permute-start.7
  184.9 4.1 copy-start.25
  185.1 4.2 copy-start.23
  192.8 217.3 %copy-start = (f32[1,32,1024]{2,1,0:T(8,128)}, f32[1,32,1024]{2,1,0:T(8,128)S(1)}, u32[]{:S(2)}) copy-start(f32[1,32,1024]{2,1,0:T(8,128)S(1)} %fusion.44) | copy-start | bytes 393220
  192.8 65.0 %copy-start.31 = (s32[8192]{0:T(1024)S(1)}, s32[8192]{0:T(1024)}, u32[]{:S(2)}) copy-start(s32[8192]{0:T(1024)} %param.16) | copy-start | bytes 98308
  (13 other events, 14.2 us)
Sparse Core Ops, SparseCore 0:
  21.8 68.5 all-gather.2
  116.6 63.0 all-gather.4
  418.5 436.9 all-reduce.11
